TPU v7x, 32 devices: a whole 2x2x4 slice. The times are simulated.
32 devices in a mesh: dp: 2 (over y), ctx: 4 (over z), wt: 4 (over x, core).
Axes of the slice: x: 2, y: 2, z: 4, core: 2. Of those that a mesh axis runs over, the one named last changes fastest.
Arguments:
- hidden: bfloat16 [8, 512, 1024], P(('dp', 'wt'), 'ctx'), may hold values from -6 to 6
- lengths: int32 [8], P(('dp', 'wt')), may hold values from 128 to 512, as said below
- buckets: int32 [1023], replicated, may hold values from 0 to 511, as said below
- w_query: bfloat16 [1024, 1024], P('wt'), may hold values from -0.1875 to 0.1875
- w_key: bfloat16 [1024, 1024], P('wt'), may hold values from -0.1875 to 0.1875
- w_value: bfloat16 [1024, 1024], P('wt'), may hold values from -0.1875 to 0.1875
- w_output: bfloat16 [1024, 1024], P('wt'), may hold values from -0.5 to 0.5
- b_query: float32 [1024], replicated, may hold values from -3 to 3
- b_key: float32 [1024], replicated, may hold values from -3 to 3
- b_value: float32 [1024], replicated, may hold values from -3 to 3
- b_output: float32 [1024], replicated, may hold values from -3 to 3
- rel_table: bfloat16 [512, 1024], P('wt'), may hold values from -6 to 6
- gain_attn: float32 [1024], replicated, may hold values from 0.5 to 1.5
- shift_attn: float32 [1024], replicated, may hold values from -1.2 to 1.2
- w_inner: bfloat16 [1024, 4096], P('wt'), may hold values from -0.1875 to 0.1875
- b_inner: float32 [4096], replicated, may hold values from -3 to 3
- w_outer: bfloat16 [4096, 1024], P('wt'), may hold values from -0.125 to 0.125
- b_outer: float32 [1024], replicated, may hold values from -3 to 3
- gain_ffn: float32 [1024], replicated, may hold values from 0.5 to 1.5
- shift_ffn: float32 [1024], replicated, may hold values from -1.2 to 1.2
- cotangent: bfloat16 [8, 512, 1024], P(('dp', 'wt'), 'ctx'), may hold values from -6 to 6
Outputs:
- output: bfloat16 [8, 512, 1024], P(('dp', 'wt'), 'ctx')
- grad_hidden: bfloat16 [8, 512, 1024], P(('dp', 'wt'), 'ctx')
- grad_w_query: float32 [1024, 1024], P('wt')
- grad_w_key: float32 [1024, 1024], P('wt')
- grad_w_value: float32 [1024, 1024], P('wt')
- grad_w_output: float32 [1024, 1024], P('wt')
- grad_b_query: float32 [1024], P('wt')
- grad_b_key: float32 [1024], P('wt')
- grad_b_value: float32 [1024], P('wt')
- grad_b_output: float32 [1024], P('wt')
- grad_rel_table: float32 [512, 1024], P('wt')
- grad_gain_attn: float32 [1024], P('wt')
- grad_shift_attn: float32 [1024], P('wt')
- grad_w_inner: float32 [1024, 4096], P('wt')
- grad_b_inner: float32 [4096], P('wt')
- grad_w_outer: float32 [4096, 1024], P('wt')
- grad_b_outer: float32 [1024], P('wt')
- grad_gain_ffn: float32 [1024], P('wt')
- grad_shift_ffn: float32 [1024], P('wt')
Inputs may be any that keep to these rules, and one draw needn't show every extreme that they name: lengths[n] is the number of valid leading slots of sequence n; one sequence has exactly 512 and another exactly 128. buckets[r + 511] is the bucket of relative distance r = i - j; it never falls as r rises, equals 256 + r for |r| <= 128, and is 0 at r = 1 - 512 and 511 at r = 511.
All inputs are finite; a program needn't handle non-finite values.
Results may differ from a plain program's by a relative error of at most 0.03.
Values may be sent and summed in bfloat16 or wider, within the bound.
A program may use at most 320 MiB of HBM per device.

v0:
```python
from functools import partial
import math

import jax
import jax.numpy as jnp
from jax import lax
from jax.sharding import PartitionSpec as P

HEADS = 16
HEAD_DIM = 64


EPSILON = 1e-07


def matmul(left_side, right_side):
    return jnp.dot(left_side, right_side, preferred_element_type=jnp.float32)


def contract_rows(left_side, right_side):
    return lax.dot_general(
        left_side, right_side, (((0,), (0,)), ((), ())), preferred_element_type=jnp.float32
    )


def contract_cols(left_side, right_side):
    return lax.dot_general(
        left_side, right_side, (((1,), (1,)), ((), ())), preferred_element_type=jnp.float32
    )


def normalize(values_in, gain_row, shift_row):
    row_mean = jnp.mean(values_in, axis=-1, keepdims=True)
    centred = values_in - row_mean
    row_var = jnp.mean(centred * centred, axis=-1, keepdims=True)
    return centred * lax.rsqrt(row_var + EPSILON) * gain_row + shift_row


def skew(table, row_count, col_count):
    head_count = table.shape[0]
    width = table.shape[2]
    flat = table.reshape(head_count, row_count * width)
    cut = lax.slice_in_dim(flat, row_count - 1, row_count - 1 + row_count * (width - 1), axis=1)
    return cut.reshape(head_count, row_count, width - 1)[:, :, :col_count]


def unskew(grad_block, row_count, col_count):
    head_count = grad_block.shape[0]
    width = row_count + col_count - 1
    padded = jnp.pad(grad_block, ((0, 0), (0, 0), (0, width - 1 - col_count)))
    flat = padded.reshape(head_count, row_count * (width - 1))
    flat = jnp.pad(flat, ((0, 0), (row_count - 1, 1)))
    return flat.reshape(head_count, row_count, width)


def distance_buckets(buckets, start, width):
    return jnp.flip(lax.dynamic_slice_in_dim(buckets, start, width, 0))


def block_terms(
    query_h, key_block, rel_key_h, rel_query_h, buckets, first_slot, key_start, slot_count
):
    row_count = query_h.shape[0]
    col_count = key_block.shape[0]
    width = row_count + col_count - 1
    along_index = distance_buckets(buckets, first_slot - key_start + slot_count - col_count, width)
    across_index = distance_buckets(buckets, key_start - first_slot + slot_count - row_count, width)
    rel_key_rows = jnp.take(rel_key_h, along_index, axis=0)
    rel_query_rows = jnp.take(rel_query_h, across_index, axis=0)
    content = jnp.einsum("qhd,khd->hqk", query_h, key_block, preferred_element_type=jnp.float32)
    along = jnp.einsum("qhd,shd->hqs", query_h, rel_key_rows, preferred_element_type=jnp.float32)
    across = jnp.einsum(
        "khd,shd->hks", key_block, rel_query_rows, preferred_element_type=jnp.float32
    )
    raw = (
        content
        + skew(along, row_count, col_count)
        + jnp.transpose(skew(across, col_count, row_count), (0, 2, 1))
    )
    return (raw, along_index, across_index)


def all_scores(query_h, key_h, rel_key_h, rel_query_h, buckets, first_slot, score_scale, key_valid):
    slot_count = key_h.shape[0]
    raw_block, along_index, across_index = block_terms(
        query_h, key_h, rel_key_h, rel_query_h, buckets, first_slot, 0, slot_count
    )
    index_parts = [(along_index, across_index)]
    scores = jnp.where(key_valid, raw_block * score_scale, -1000000000.0)
    return (scores, index_parts)


def column_sum(grad_rows):
    return jnp.sum(grad_rows.astype(jnp.float32), axis=0)


def per_device(
    hidden,
    lengths,
    buckets,
    w_query,
    w_key,
    w_value,
    w_output,
    b_query,
    b_key,
    b_value,
    b_output,
    rel_table,
    gain_attn,
    shift_attn,
    w_inner,
    b_inner,
    w_outer,
    b_outer,
    gain_ffn,
    shift_ffn,
    cotangent,
):
    gathered = (
        lax.all_gather(w_query, "wt", axis=0, tiled=True),
        lax.all_gather(w_key, "wt", axis=0, tiled=True),
        lax.all_gather(w_value, "wt", axis=0, tiled=True),
        lax.all_gather(w_output, "wt", axis=0, tiled=True),
        lax.all_gather(w_inner, "wt", axis=0, tiled=True),
        lax.all_gather(w_outer, "wt", axis=0, tiled=True),
        lax.all_gather(rel_table, "wt", axis=0, tiled=True),
    )
    full_query, full_key, full_value, full_output, full_inner, full_outer, full_rel = gathered
    tokens = hidden[0]
    token_rows = tokens.shape[0]
    model_width = tokens.shape[1]
    score_scale = 1.0 / math.sqrt(3 * HEAD_DIM)
    first_slot = lax.axis_index("ctx") * token_rows
    seq_length = lengths[0]
    query_low = (matmul(tokens, full_query) + b_query).astype(jnp.bfloat16)
    key_low = (matmul(tokens, full_key) + b_key).astype(jnp.bfloat16)
    value_low = (matmul(tokens, full_value) + b_value).astype(jnp.bfloat16)
    rel_key = (matmul(full_rel, full_key) + b_key).astype(jnp.bfloat16)
    rel_query = (matmul(full_rel, full_query) + b_query).astype(jnp.bfloat16)
    all_keys, all_values = (
        lax.all_gather(key_low, "ctx", axis=0, tiled=True),
        lax.all_gather(value_low, "ctx", axis=0, tiled=True),
    )
    slot_count = all_keys.shape[0]
    key_width = math.gcd(slot_count, 512)
    bucket_count = rel_key.shape[0]
    query_pos = first_slot + jnp.arange(token_rows, dtype=jnp.int32)
    key_pos = jnp.arange(slot_count, dtype=jnp.int32)
    key_valid = (key_pos < seq_length)[None, None, :]
    query_h = query_low.reshape(token_rows, HEADS, HEAD_DIM)
    key_h = all_keys.reshape(slot_count, HEADS, HEAD_DIM)
    value_h = all_values.reshape(slot_count, HEADS, HEAD_DIM)
    rel_key_h = rel_key.reshape(bucket_count, HEADS, HEAD_DIM)
    rel_query_h = rel_query.reshape(bucket_count, HEADS, HEAD_DIM)
    scores, index_parts = all_scores(
        query_h, key_h, rel_key_h, rel_query_h, buckets, first_slot, score_scale, key_valid
    )
    row_top = jnp.max(scores, axis=2, keepdims=True)
    exponent = jnp.exp(scores - row_top)
    row_mass = jnp.sum(exponent, axis=2, keepdims=True)
    probs_low = (exponent / row_mass).astype(jnp.bfloat16)
    log_total = row_top + jnp.log(row_mass)
    context = jnp.einsum("hqk,khd->qhd", probs_low, value_h, preferred_element_type=jnp.float32)
    context = context.reshape(token_rows, model_width).astype(jnp.bfloat16)
    residual_one = tokens.astype(jnp.float32) + matmul(context, full_output) + b_output
    normed_one = normalize(residual_one, gain_attn, shift_attn)
    normed_low = normed_one.astype(jnp.bfloat16)
    inner_pre = matmul(normed_low, full_inner) + b_inner
    active_low = jax.nn.gelu(inner_pre, approximate=False).astype(jnp.bfloat16)
    residual_two = normed_one + matmul(active_low, full_outer) + b_outer
    result = normalize(residual_two, gain_ffn, shift_ffn)
    regathered = (
        lax.all_gather(w_query, "wt", axis=0, tiled=True),
        lax.all_gather(w_key, "wt", axis=0, tiled=True),
        lax.all_gather(w_value, "wt", axis=0, tiled=True),
        lax.all_gather(w_output, "wt", axis=0, tiled=True),
        lax.all_gather(w_inner, "wt", axis=0, tiled=True),
        lax.all_gather(w_outer, "wt", axis=0, tiled=True),
        lax.all_gather(rel_table, "wt", axis=0, tiled=True),
    )
    full_query, full_key, full_value, full_output, full_inner, full_outer, full_rel = regathered
    slot_valid = (query_pos < seq_length).astype(jnp.float32)
    seed_grad = cotangent[0].astype(jnp.float32) * slot_valid[:, None]
    norm_two_back = jax.vjp(normalize, residual_two, gain_ffn, shift_ffn)[1]
    d_res_two, grad_gain_ffn, grad_shift_ffn = norm_two_back(seed_grad)
    d_branch = d_res_two.astype(jnp.bfloat16)
    d_active = contract_cols(d_branch, full_outer)
    gelu_back = jax.vjp(partial(jax.nn.gelu, approximate=False), inner_pre)[1]
    d_inner = gelu_back(d_active)[0].astype(jnp.bfloat16)
    d_normed = d_res_two + contract_cols(d_inner, full_inner)
    norm_one_back = jax.vjp(normalize, residual_one, gain_attn, shift_attn)[1]
    d_res_one, grad_gain_attn, grad_shift_attn = norm_one_back(d_normed)
    d_attn = d_res_one.astype(jnp.bfloat16)
    d_context = contract_cols(d_attn, full_output).astype(jnp.bfloat16)
    d_context_h = d_context.reshape(token_rows, HEADS, HEAD_DIM)
    scores, index_parts = all_scores(
        query_h, key_h, rel_key_h, rel_query_h, buckets, first_slot, score_scale, key_valid
    )
    probs_full = jnp.exp(scores - log_total)
    d_probs = jnp.einsum("qhd,khd->hqk", d_context_h, value_h, preferred_element_type=jnp.float32)
    d_value_part = jnp.einsum(
        "hqk,qhd->khd", probs_low, d_context_h, preferred_element_type=jnp.float32
    )
    row_inner = jnp.sum(probs_full * d_probs, axis=2, keepdims=True)
    d_scores = (probs_full * (d_probs - row_inner) * score_scale).astype(jnp.bfloat16)
    d_query_sum = jnp.einsum("hqk,khd->qhd", d_scores, key_h, preferred_element_type=jnp.float32)
    d_key_part = jnp.einsum("hqk,qhd->khd", d_scores, query_h, preferred_element_type=jnp.float32)
    bucket_ids = jnp.arange(bucket_count, dtype=jnp.int32)
    d_along_sum = jnp.zeros((HEADS, token_rows, bucket_count), jnp.float32)
    d_rel_query = jnp.zeros((bucket_count, HEADS, HEAD_DIM), jnp.float32)
    key_rel_parts = []
    for block_number, key_start in enumerate(range(0, slot_count, key_width)):
        along_index, across_index = index_parts[block_number]
        along_hot = (along_index[:, None] == bucket_ids[None, :]).astype(jnp.bfloat16)
        across_hot = (across_index[:, None] == bucket_ids[None, :]).astype(jnp.bfloat16)
        d_along_sum = jnp.einsum(
            "hqs,sb->hqb",
            unskew(d_scores, token_rows, key_width),
            along_hot,
            preferred_element_type=jnp.float32,
        )
        flipped = jnp.transpose(d_scores, (0, 2, 1))
        d_across_block = jnp.einsum(
            "hks,sb->hkb",
            unskew(flipped, key_width, token_rows),
            across_hot,
            preferred_element_type=jnp.float32,
        ).astype(jnp.bfloat16)
        key_rel_parts.append(
            jnp.einsum(
                "hkr,rhd->khd", d_across_block, rel_query_h, preferred_element_type=jnp.float32
            )
        )
        d_rel_query = jnp.einsum(
            "hkr,khd->rhd", d_across_block, key_h, preferred_element_type=jnp.float32
        )
    d_along = d_along_sum.astype(jnp.bfloat16)
    d_query_sum = d_query_sum + jnp.einsum(
        "hqr,rhd->qhd", d_along, rel_key_h, preferred_element_type=jnp.float32
    )
    d_key_part = d_key_part + key_rel_parts[0]
    d_rel_key = jnp.einsum("hqr,qhd->rhd", d_along, query_h, preferred_element_type=jnp.float32)
    d_key_sum, d_value_sum = (
        lax.psum_scatter(
            d_key_part.reshape(slot_count, model_width).astype(jnp.bfloat16),
            "ctx",
            scatter_dimension=0,
            tiled=True,
        ).astype(jnp.float32),
        lax.psum_scatter(
            d_value_part.reshape(slot_count, model_width).astype(jnp.bfloat16),
            "ctx",
            scatter_dimension=0,
            tiled=True,
        ).astype(jnp.float32),
    )
    d_query_low = d_query_sum.reshape(token_rows, model_width).astype(jnp.bfloat16)
    d_key_low = d_key_sum.astype(jnp.bfloat16)
    d_value_low = d_value_sum.astype(jnp.bfloat16)
    grad_tokens = (
        d_res_one
        + contract_cols(d_query_low, full_query)
        + contract_cols(d_key_low, full_key)
        + contract_cols(d_value_low, full_value)
    )
    rel_key_sum, rel_query_sum = lax.psum(
        (
            d_rel_key.reshape(bucket_count, model_width),
            d_rel_query.reshape(bucket_count, model_width),
        ),
        ("dp", "ctx", "wt"),
    )
    rel_key_grad = rel_key_sum.astype(jnp.bfloat16)
    rel_query_grad = rel_query_sum.astype(jnp.bfloat16)
    partial_grads = (
        contract_rows(tokens, d_query_low),
        contract_rows(tokens, d_key_low),
        contract_rows(tokens, d_value_low),
        contract_rows(context, d_attn),
        contract_rows(normed_low, d_inner),
        contract_rows(active_low, d_branch),
        column_sum(d_query_low),
        column_sum(d_key_low),
        column_sum(d_value_low),
        column_sum(d_attn),
        column_sum(d_inner),
        column_sum(d_branch),
        grad_gain_attn,
        grad_shift_attn,
        grad_gain_ffn,
        grad_shift_ffn,
    )
    shard_grads = (
        lax.psum_scatter(
            partial_grads[0].astype(jnp.bfloat16), "wt", scatter_dimension=0, tiled=True
        ).astype(jnp.float32),
        lax.psum_scatter(
            partial_grads[1].astype(jnp.bfloat16), "wt", scatter_dimension=0, tiled=True
        ).astype(jnp.float32),
        lax.psum_scatter(
            partial_grads[2].astype(jnp.bfloat16), "wt", scatter_dimension=0, tiled=True
        ).astype(jnp.float32),
        lax.psum_scatter(
            partial_grads[3].astype(jnp.bfloat16), "wt", scatter_dimension=0, tiled=True
        ).astype(jnp.float32),
        lax.psum_scatter(
            partial_grads[4].astype(jnp.bfloat16), "wt", scatter_dimension=0, tiled=True
        ).astype(jnp.float32),
        lax.psum_scatter(
            partial_grads[5].astype(jnp.bfloat16), "wt", scatter_dimension=0, tiled=True
        ).astype(jnp.float32),
        lax.psum_scatter(
            partial_grads[6].astype(jnp.bfloat16), "wt", scatter_dimension=0, tiled=True
        ).astype(jnp.float32),
        lax.psum_scatter(
            partial_grads[7].astype(jnp.bfloat16), "wt", scatter_dimension=0, tiled=True
        ).astype(jnp.float32),
        lax.psum_scatter(
            partial_grads[8].astype(jnp.bfloat16), "wt", scatter_dimension=0, tiled=True
        ).astype(jnp.float32),
        lax.psum_scatter(
            partial_grads[9].astype(jnp.bfloat16), "wt", scatter_dimension=0, tiled=True
        ).astype(jnp.float32),
        lax.psum_scatter(
            partial_grads[10].astype(jnp.bfloat16), "wt", scatter_dimension=0, tiled=True
        ).astype(jnp.float32),
        lax.psum_scatter(
            partial_grads[11].astype(jnp.bfloat16), "wt", scatter_dimension=0, tiled=True
        ).astype(jnp.float32),
        lax.psum_scatter(
            partial_grads[12].astype(jnp.bfloat16), "wt", scatter_dimension=0, tiled=True
        ).astype(jnp.float32),
        lax.psum_scatter(
            partial_grads[13].astype(jnp.bfloat16), "wt", scatter_dimension=0, tiled=True
        ).astype(jnp.float32),
        lax.psum_scatter(
            partial_grads[14].astype(jnp.bfloat16), "wt", scatter_dimension=0, tiled=True
        ).astype(jnp.float32),
        lax.psum_scatter(
            partial_grads[15].astype(jnp.bfloat16), "wt", scatter_dimension=0, tiled=True
        ).astype(jnp.float32),
    )
    total_grads = lax.psum(
        (
            shard_grads[0],
            shard_grads[1],
            shard_grads[2],
            shard_grads[3],
            shard_grads[4],
            shard_grads[5],
            shard_grads[6],
            shard_grads[7],
            shard_grads[8],
            shard_grads[9],
            shard_grads[10],
            shard_grads[11],
            shard_grads[12],
            shard_grads[13],
            shard_grads[14],
            shard_grads[15],
        ),
        ("dp", "ctx"),
    )
    wt_index = lax.axis_index("wt")
    shard_width = model_width // lax.axis_size("wt")
    col_start = wt_index * shard_width
    rel_cols = lax.dynamic_slice_in_dim(full_rel, col_start, shard_width, 1)
    grad_w_query = total_grads[0] + contract_rows(rel_cols, rel_query_grad)
    grad_w_key = total_grads[1] + contract_rows(rel_cols, rel_key_grad)
    bucket_shard = rel_table.shape[0]
    row_start = wt_index * bucket_shard
    key_rows = lax.dynamic_slice_in_dim(rel_key_grad, row_start, bucket_shard, 0)
    query_rows = lax.dynamic_slice_in_dim(rel_query_grad, row_start, bucket_shard, 0)
    grad_rel = contract_cols(key_rows, full_key) + contract_cols(query_rows, full_query)
    grad_b_query = total_grads[6] + lax.dynamic_slice_in_dim(
        column_sum(rel_query_grad), col_start, shard_width, 0
    )
    grad_b_key = total_grads[7] + lax.dynamic_slice_in_dim(
        column_sum(rel_key_grad), col_start, shard_width, 0
    )
    return (
        result.astype(jnp.bfloat16)[None],
        grad_tokens.astype(jnp.bfloat16)[None],
        grad_w_query,
        grad_w_key,
        total_grads[2],
        total_grads[3],
        grad_b_query,
        grad_b_key,
        total_grads[8],
        total_grads[9],
        grad_rel,
        total_grads[12],
        total_grads[13],
        total_grads[4],
        total_grads[10],
        total_grads[5],
        total_grads[11],
        total_grads[14],
        total_grads[15],
    )


def solution(mesh):
    in_specs = (
        P(("dp", "wt"), "ctx", None),
        P(("dp", "wt")),
        P(),
        P("wt", None),
        P("wt", None),
        P("wt", None),
        P("wt", None),
        P(),
        P(),
        P(),
        P(),
        P("wt", None),
        P(),
        P(),
        P("wt", None),
        P(),
        P("wt", None),
        P(),
        P(),
        P(),
        P(("dp", "wt"), "ctx", None),
    )
    out_specs = (
        P(("dp", "wt"), "ctx", None),
        P(("dp", "wt"), "ctx", None),
        P("wt", None),
        P("wt", None),
        P("wt", None),
        P("wt", None),
        P("wt"),
        P("wt"),
        P("wt"),
        P("wt"),
        P("wt", None),
        P("wt"),
        P("wt"),
        P("wt", None),
        P("wt"),
        P("wt", None),
        P("wt"),
        P("wt"),
        P("wt"),
    )
    return jax.shard_map(
        per_device, mesh=mesh, in_specs=in_specs, out_specs=out_specs, check_vma=False
    )
```

profile of v0, /device:TPU:0, one launch (start us, length us, event | category | flops | bytes accessed | tf_op | source)
XLA Modules:
  0.0 1274.5 jit_solution(7010836301278323304)
XLA Ops:
  10.1 24.8 %all-gather.16.cloned.1.call-done = bf16[1024,1024]{1,0:T(8,128)(2,1)} async-done(((bf16[256,1024]{1,0:T(8,128)(2,1)}), bf16[1024,1024]{1,0:T(8,128)(2,1)}) %all-gather.16.cloned.1.call-update) | async-done | bytes 2097168 | tf_op jit(solution)/shard_map/all_gather | solution.py:122
  34.9 2.7 fusion.28
  37.7 21.4 %all-gather.10.cloned.1.call-done = bf16[1024,1024]{1,0:T(8,128)(2,1)} async-done(((bf16[256,1024]{1,0:T(8,128)(2,1)}), bf16[1024,1024]{1,0:T(8,128)(2,1)}) %all-gather.10.cloned.1.call-update) | async-done | bytes 2097168 | tf_op jit(solution)/shard_map/all_gather | solution.py:123
  59.1 2.7 fusion.26
  65.9 11.5 all-gather.20.cloned.1.call-done
  77.4 24.0 %all-gather.14.cloned.1.call-done = bf16[1024,1024]{1,0:T(8,128)(2,1)} async-done(((bf16[256,1024]{1,0:T(8,128)(2,1)}), bf16[1024,1024]{1,0:T(8,128)(2,1)}) %all-gather.14.cloned.1.call-update) | async-done | bytes 2097168 | tf_op jit(solution)/shard_map/all_gather | solution.py:121
  101.4 3.2 add_convert_fusion.2
  105.2 2.8 copy.83
  108.1 3.5 add_convert_fusion.3
  113.0 2.8 copy.80
  117.0 1.8 copy.77
  118.8 3.0 gather_fusion
  121.8 2.3 broadcast_select_fusion.1
  124.1 3.6 fusion.10
  127.7 6.1 reshape.204
  133.8 6.2 slice.24
  140.1 9.6 reshape.205
  149.7 3.3 gather_fusion.1
  153.0 5.1 broadcast_select_fusion
  159.6 11.0 fusion.8
  170.5 28.3 %reshape.207 = f32[16,327168]{1,0:T(8,128)} reshape(f32[16,512,639]{2,1,0:T(8,128)} %fusion.8) | data formatting | bytes 41877504 | tf_op jit(solution)/shard_map/reshape | solution.py:42
  198.8 18.1 %slice.26 = f32[16,326656]{1,0:T(8,128)} slice(f32[16,327168]{1,0:T(8,128)} %reshape.207), slice={[0:16], [511:327167]} | slice | bytes 41811968 | tf_op jit(solution)/shard_map/slice | solution.py:43
  216.9 40.9 %reshape.208 = f32[16,512,638]{2,1,0:T(8,128)} reshape(f32[16,326656]{1,0:T(8,128)} %slice.26) | data formatting | bytes 41811968 | tf_op jit(solution)/shard_map/reshape | solution.py:44
  257.8 4.9 slice.27
  262.8 5.7 copy.101
  270.1 5.0 fusion.70
  280.3 2.3 fusion.71
  283.0 9.6 multiply_convert_fusion.1
  292.6 11.7 all-gather.26.cloned.1.call-done
  304.3 4.9 fusion.72
  311.1 5.3 fusion.64
  316.4 3.2 multiply_reduce_fusion.1
  323.1 1.8 copy.86
  324.9 2.4 convolution_convert_fusion.5
  327.2 8.9 multiply_convert_fusion
  336.1 2.8 copy.102
  338.9 7.0 pad.18.clone
  345.9 27.5 %reshape.212 = bf16[16,326656]{1,0:T(8,128)(2,1)} reshape(bf16[16,512,638]{2,1,0:T(8,128)(2,1)} %pad.18.clone) | data formatting | bytes 20905984 | tf_op jit(solution)/shard_map/reshape | solution.py:51
  373.4 11.0 pad.19
  384.4 34.8 %reshape.213 = bf16[16,512,639]{2,1,0:T(8,128)(2,1)} reshape(bf16[16,327168]{1,0:T(8,128)(2,1)} %pad.19) | data formatting | bytes 20938752 | tf_op jit(solution)/shard_map/reshape | solution.py:53
  419.2 2.3 copy.97
  422.9 11.2 convolution_convert_fusion.2
  434.1 3.7 add_convert_fusion
  437.9 2.3 copy.95
  440.2 3.1 convolution_convert_fusion.4
  443.4 1.8 pad.16
  445.2 6.6 reshape.210
  451.8 4.0 pad.17
  455.7 8.4 reshape.211
  465.9 1.9 convolution_convert_fusion.3
  469.8 2.0 convert_bitcast_fusion.2
  471.9 3.0 convert_bitcast_fusion
  475.0 2.5 reduce-scatter.25.cloned.1.call-done
  477.6 3.0 convert_bitcast_fusion.1
  480.7 6.0 convolution_convert_fusion
  488.1 5.7 convolution_convert_fusion.1
  496.4 5.1 fusion.75
  503.4 101.2 %all-reduce.19 = (bf16[512,1024]{0,1:T(8,128)(2,1)S(1)}, bf16[512,1024]{0,1:T(8,128)(2,1)}) all-reduce(f32[512,1024]{0,1:T(8,128)S(1)} %bitcast.142, f32[512,1024]{0,1:T(8,128)} %bitcast.149), channel_id=1, replica_groups=mesh['dp'=2,'ctx'=4,'wt'=4] {'dp','ctx','wt'}, use_global_device_ids=true, to_apply=%region_15.17 | all-reduce | flops 1048576 | bytes 6291456 | tf_op jit(solution)/shard_map/psum | solution.py:267
  612.7 10.8 all-reduce.16
  623.9 2.1 convolution_add_fusion.6
  627.7 65.9 %reduce-scatter.23.cloned.1.call-done = bf16[1024,1024]{1,0:T(8,128)(2,1)} async-done(((bf16[4096,1024]{1,0:T(8,128)(2,1)}), bf16[1024,1024]{1,0:T(8,128)(2,1)}) %reduce-scatter.23.cloned.1.call-update) | async-done | bytes 2097168 | tf_op jit(solution)/shard_map/reduce_scatter | solution.py:310
  693.6 74.3 %reduce-scatter.21.cloned.1.call-done = bf16[256,4096]{1,0:T(8,128)(2,1)} async-done(((bf16[1024,4096]{1,0:T(8,128)(2,1)}), bf16[256,4096]{1,0:T(8,128)(2,1)}) %reduce-scatter.21.cloned.1.call-update) | async-done | bytes 2097168 | tf_op jit(solution)/shard_map/reduce_scatter | solution.py:307
  767.9 491.0 %all-reduce.20 = (f32[256,1024]{0,1:T(8,128)}, f32[256,1024]{0,1:T(8,128)}, f32[256,1024]{0,1:T(8,128)}, f32[256,1024]{1,0:T(8,128)}, f32[256]{0:T(256)S(1)}, /*...) all-reduce(bf16[256,1024]{0,1:T(8,128)(2,1)} %reduce-scatter.13.clo, ...), channel_id=1, replica_groups=mesh['dp'=2,'ctx'=4,'wt'=4] {'dp','ctx'}, use_global_device_ids=true, to_apply=%region_14.16 | all-reduce | flops 3149056 | bytes 18900992 | tf_op jit(solution)/shard_map/psum | solution.py:344
  1262.0 1.8 convolution_add_fusion.2
  (226 shorter events, 50.0 us)
Async XLA Ops:
  7.2 27.7 %all-gather.16.cloned.1.call-start = ((), (), s32[]{:S(2)}) async-start(), calls=%async_computation.11 | async-start | bytes 2621440 | tf_op jit(solution)/shard_map/all_gather | solution.py:122
  7.9 51.2 %copy-start.10 = (bf16[1,128,1024]{2,1,0:T(8,128)(2,1)S(1)}, bf16[1,128,1024]{2,1,0:T(8,128)(2,1)}, u32[]{:S(2)}) copy-start(bf16[1,128,1024]{2,1,0:T(8,128)(2,1)} %param.23) | copy-start | bytes 786436
  7.9 51.2 %copy-start.47 = (f32[1024]{0:T(1024)S(1)}, f32[1024]{0:T(1024)}, u32[]{:S(2)}) copy-start(f32[1024]{0:T(1024)} %param.32) | copy-start | bytes 12292
  7.9 51.1 %all-gather.10.cloned.1.call-start = ((), (), s32[]{:S(2)}) async-start(), calls=%async_computation.8 | async-start | bytes 2621440 | tf_op jit(solution)/shard_map/all_gather | solution.py:123
  8.7 68.7 %all-gather.20.cloned.1.call-start = ((), (), s32[]{:S(2)}) async-start(), calls=%async_computation.13 | async-start | bytes 1310720 | tf_op jit(solution)/shard_map/all_gather | solution.py:127
  9.4 92.0 %all-gather.14.cloned.1.call-start = ((), (), s32[]{:S(2)}) async-start(), calls=%async_computation.10 | async-start | bytes 2621440 | tf_op jit(solution)/shard_map/all_gather | solution.py:121
  10.0 148.1 %all-gather.18.cloned.1.call-start = ((), (), s32[]{:S(2)}) async-start(), calls=%async_computation.12 | async-start | bytes 1310720 | tf_op jit(solution)/shard_map/all_gather | solution.py:142
  37.7 230.8 %all-gather.12.cloned.1.call-start = ((), (), s32[]{:S(2)}) async-start(), calls=%async_computation.9 | async-start | bytes 1310720 | tf_op jit(solution)/shard_map/all_gather | solution.py:143
  61.9 218.5 %all-gather.22.cloned.1.call-start = ((), (), s32[]{:S(2)}) async-start(), calls=%async_computation.14 | async-start | bytes 2621440 | tf_op jit(solution)/shard_map/all_gather | solution.py:124
  62.6 38.8 %copy-start.49 = (f32[1024]{0:T(1024)S(1)}, f32[1024]{0:T(1024)}, u32[]{:S(2)}) copy-start(f32[1024]{0:T(1024)} %param.30) | copy-start | bytes 12292
  62.6 220.3 %all-gather.24.cloned.1.call-start = ((), (), s32[]{:S(2)}) async-start(), calls=%async_computation.15 | async-start | bytes 10485760 | tf_op jit(solution)/shard_map/all_gather | solution.py:125
  63.4 240.9 %all-gather.26.cloned.1.call-start = ((), (), s32[]{:S(2)}) async-start(), calls=%async_computation.16 | async-start | bytes 10485760 | tf_op jit(solution)/shard_map/all_gather | solution.py:126
  64.1 407.8 %reduce-scatter.27.cloned.1.call-start = ((), (), s32[]{:S(2)}) async-start(), calls=%async_computation.24 | async-start | bytes 1310720
  105.2 2.9 copy-start.16
  105.2 2.9 copy-start.6
  105.2 2.9 copy-start.48
  113.0 4.0 copy-start.14
  113.0 2.9 copy-start.4
  121.8 2.3 copy-start.22
  140.1 9.6 copy-start.13
  270.1 8.0 copy-start.28
  275.1 2.0 copy-start.1
  278.0 2.3 copy-start.50
  280.3 2.6 copy-start.36
  280.3 2.7 copy-start.41
  280.3 2.7 copy-start.42
  280.3 2.7 copy-start.53
  282.6 37.0 %copy-start.2 = (f32[128,1024]{1,0:T(8,128)}, f32[128,1024]{1,0:T(8,128)S(1)}, u32[]{:S(2)}) copy-start(f32[128,1024]{1,0:T(8,128)S(1)} %get-tuple-element.133) | copy-start | bytes 1572868
  282.9 21.4 %copy-start.52 = (f32[1024]{0:T(1024)S(1)}, f32[1024]{0:T(1024)}, u32[]{:S(2)}) copy-start(f32[1024]{0:T(1024)} %param.40) | copy-start | bytes 12292
  292.6 16.7 %copy-start.11 = (bf16[128,4096]{1,0:T(8,128)(2,1)}, bf16[128,4096]{1,0:T(8,128)(2,1)S(1)}, u32[]{:S(2)}) copy-start(bf16[128,4096]{1,0:T(8,128)(2,1)S(1)} %get-tuple-element.121) | copy-start | bytes 3145732
  304.3 6.7 slice-start
  304.3 5.2 copy-start.38
  304.3 5.2 copy-start.43
  304.3 5.6 copy-start.51
  304.3 6.7 slice-start.1
  309.3 1.8 copy-start.55
  309.9 6.5 slice-start.2
  311.0 5.4 copy-start.39
  311.1 5.3 slice-start.3
  316.4 3.2 copy-start.29
  319.6 2.0 copy-start.19
  319.9 5.0 copy-start.9
  421.5 56.1 %reduce-scatter.25.cloned.1.call-start = ((), (), s32[]{:S(2)}) async-start(), calls=%async_computation.23 | async-start | bytes 1310720
  422.9 11.2 copy-start.17
  434.1 3.7 copy-start
  440.2 187.5 %reduce-scatter.19.cloned.1.call-start = ((), (), s32[]{:S(2)}) async-start(), calls=%async_computation.20 | async-start | bytes 2621440 | tf_op jit(solution)/shard_map/reduce_scatter | solution.py:304
  443.3 184.3 %reduce-scatter.13.cloned.1.call-start = ((), (), s32[]{:S(2)}) async-start(), calls=%async_computation.17 | async-start | bytes 2621440 | tf_op jit(solution)/shard_map/reduce_scatter | solution.py:295
  464.1 1.8 copy-start.31
  464.1 1.8 copy-start.46
  465.9 1.9 copy-start.15
  471.8 155.8 %reduce-scatter.17.cloned.1.call-start = ((), (), s32[]{:S(2)}) async-start(), calls=%async_computation.19 | async-start | bytes 2621440 | tf_op jit(solution)/shard_map/reduce_scatter | solution.py:301
  475.0 5.7 copy-start.12
  475.0 5.7 copy-start.40
  475.0 152.7 %reduce-scatter.15.cloned.1.call-start = ((), (), s32[]{:S(2)}) async-start(), calls=%async_computation.18 | async-start | bytes 2621440 | tf_op jit(solution)/shard_map/reduce_scatter | solution.py:298
  480.6 213.0 %reduce-scatter.23.cloned.1.call-start = ((), (), s32[]{:S(2)}) async-start(), calls=%async_computation.22 | async-start | bytes 10485760 | tf_op jit(solution)/shard_map/reduce_scatter | solution.py:310
  486.7 281.2 %reduce-scatter.21.cloned.1.call-start = ((), (), s32[]{:S(2)}) async-start(), calls=%async_computation.21 | async-start | bytes 10485760 | tf_op jit(solution)/shard_map/reduce_scatter | solution.py:307
  496.4 5.1 copy-start.21
  496.4 5.1 copy-start.24
  604.6 2.0 copy-start.7
  604.6 3.7 copy-start.5
  608.3 1.7 copy-start.27
  623.5 2.5 copy-start.18
  767.9 491.0 %copy-start.25 = (bf16[512,1024]{0,1:T(8,128)(2,1)S(1)}, bf16[512,1024]{0,1:T(8,128)(2,1)}, u32[]{:S(2)}) copy-start(bf16[512,1024]{0,1:T(8,128)(2,1)} %get-tuple-element.84) | copy-start | bytes 3145732
  1262.0 3.1 copy-start.37
  (13 other events, 15.1 us)
Sparse Core Ops, SparseCore 0:
  9.6 25.2 all-gather.15
  36.5 22.5 all-gather.9
  60.6 16.7 all-gather.19
  78.8 22.5 all-gather.13
  103.4 27.9 all-gather.17
  133.4 27.4 all-gather.11
  162.4 22.0 all-gather.21
  186.1 58.2 all-gather.23
  246.0 58.2 all-gather.25
  421.6 27.1 reduce-scatter.26
  451.7 25.7 reduce-scatter.24
  479.9 30.0 reduce-scatter.18
  513.3 35.3 reduce-scatter.12
  551.1 32.8 reduce-scatter.16
  587.0 32.2 reduce-scatter.14
  621.8 71.7 reduce-scatter.22
  696.2 71.6 reduce-scatter.20
where the time goes:
time: 1280 us; the launch traced here: 1270 us
  blocking collectives  603 us (47%)
  local copies, waits for them, and re-layouts  262 us (20%)
  waiting for transfers between devices  241 us (19%)
  matrix products  134 us (10%)
  between operations  17.1 us (1%)
  other arithmetic  16.3 us (1%)
    psum x1, blocking collectives, per_device(): lax.psum((shard_grads[0], shard_grads[1], shard_grads[2], shard_grads[3],...  491 us
    psum x1, blocking collectives, per_device(): lax.psum((d_rel_key.reshape(bucket_count, model_width), d_rel_query.resha...  101 us
    reduce_scatter x1, waiting for transfers between devices, per_device(): lax.psum_scatter(partial_grads[4].astype(jnp.bfloat16), 'wt', scatter_dim...  74.3 us
    reduce_scatter x1, waiting for transfers between devices, per_device(): lax.psum_scatter(partial_grads[5].astype(jnp.bfloat16), 'wt', scatter_dim...  65.9 us
    reshape x2, local copies, waits for them, and re-layouts, skew(): return cut.reshape(head_count, row_count, width - 1)[:, :, :col_count]  50.5 us
    reshape x2, local copies, waits for them, and re-layouts, unskew(): return flat.reshape(head_count, row_count, width)  43.1 us
    reshape x2, local copies, waits for them, and re-layouts, skew(): flat = table.reshape(head_count, row_count * width)  34.4 us
    reshape x2, local copies, waits for them, and re-layouts, unskew(): flat = padded.reshape(head_count, row_count * (width - 1))  34.1 us
  transfers between devices with their start and end apart: 17, of which 8 were waited for; matrix products, arithmetic and copies ran while one was open for 22% of the time, Pallas kernels for 0%

commit v1 on v0

v1 whole, which is shorter than its diff:
```python
import functools
import math

import jax
import jax.numpy as jnp
from jax import lax
from jax.experimental import pallas as pl
from jax.experimental.pallas import tpu as pltpu
from jax.sharding import PartitionSpec as P_

BF=jnp.bfloat16; F32=jnp.float32
def dot(a,b): return jnp.dot(a,b,preferred_element_type=F32)
def dot_t(a,b): return lax.dot_general(a,b,(((1,),(1,)),((),())),preferred_element_type=F32)
def tdot(a,b): return lax.dot_general(a,b,(((0,),(0,)),((),())),preferred_element_type=F32)
BLK=128
HD=64

def lane_mask(half):
    lane=lax.broadcasted_iota(jnp.int32,(1,2*HD),1)
    return ((lane<HD) if half==0 else (lane>=HD))
def only(x,half):
    return jnp.where(lane_mask(half),x,jnp.zeros((),x.dtype))

def attn_fwd(q,k,v,rkf,rqf,P,across,ctx,length,slots,cols,scale):
    nb=slots//BLK
    win=slots+BLK
    for p in range(cols//(2*HD)):
        L=slice(p*2*HD,(p+1)*2*HD)
        for half in range(2):
            h=2*p+half
            def kb_body(J,c):
                r0=pl.multiple_of(J*BLK,BLK)
                w0=pl.multiple_of((nb-1-J)*BLK,BLK)
                kb=only(k[pl.ds(r0,BLK),L],half)
                b=dot_t(kb,rqf[pl.ds(w0,win),L])
                b=pltpu.roll(b,win-(BLK-1),1,stride=1,stride_axis=0)[:,:slots]
                across[:,pl.ds(r0,BLK)]=b.T
                return c
            lax.fori_loop(0,nb,kb_body,0,unroll=True)
            def qb_body(I,c):
                r0=pl.multiple_of(I*BLK,BLK)
                w0=pl.multiple_of((nb-1-I)*BLK,BLK)
                qb=only(q[pl.ds(r0,BLK),L],half)
                al=dot_t(qb,rkf[pl.ds(w0,win),L])
                al=pltpu.roll(al,win-(BLK-1),1,stride=1,stride_axis=0)[:,:slots]
                raw=dot_t(qb,k[:,L])+al+across[pl.ds(r0,BLK),:]
                valid=lax.broadcasted_iota(jnp.int32,(1,slots),1)<length
                sc=jnp.where(valid,raw*scale,-1e9)
                top=jnp.max(sc,axis=1,keepdims=True)
                e=jnp.exp(sc-top)
                pr=e/jnp.sum(e,axis=1,keepdims=True)
                P[h,pl.ds(r0,BLK),:]=pr
                c2=dot(pr.astype(BF),v[:,L])
                if half==0: ctx[pl.ds(r0,BLK),L]=c2.astype(BF)
                else: ctx[pl.ds(r0,BLK),L]=jnp.where(lane_mask(1),c2.astype(BF),ctx[pl.ds(r0,BLK),L])
                return c
            lax.fori_loop(0,nb,qb_body,0,unroll=True)

def attn_bwd(q,k,v,dctx,rks,rqs,P,ds,dq,dk,dv,grk,grq,slots,cols,scale):
    nb=slots//BLK
    win=slots+BLK
    RW=256
    ii=lax.broadcasted_iota(jnp.int32,(RW,RW),0); jj=lax.broadcasted_iota(jnp.int32,(RW,RW),1)
    flip=jnp.where(ii+jj==RW-1,1.0,0.0).astype(BF)
    def unskew(x):
        parts=[dot(x[:,c*RW:(c+1)*RW],flip) for c in range(slots//RW)][::-1]
        y=jnp.concatenate(parts+[jnp.zeros((BLK,BLK),F32)],axis=1)
        return pltpu.roll(y,0,1,stride=1,stride_axis=0).astype(BF)
    grk[...]=jnp.zeros_like(grk); grq[...]=jnp.zeros_like(grq)
    for p in range(cols//(2*HD)):
        L=slice(p*2*HD,(p+1)*2*HD)
        dq2=None
        for half in range(2):
            h=2*p+half
            kh=only(k[:,L],half);
            def qb_body(I,c):
                r0=pl.multiple_of(I*BLK,BLK)
                rows=pl.ds(r0,BLK)
                qb=only(q[rows,L],half)
                db=only(dctx[rows,L],half)
                dp=dot_t(db,v[:,L])
                pr=P[h,rows,:]
                ri=jnp.sum(pr*dp,axis=1,keepdims=True)
                d=(pr*(dp-ri)*scale).astype(BF)
                ds[rows,:]=d
                u=unskew(d)
                w=pl.ds(r0,win)
                g=dot(d,kh)+dot(u,only(rks[w,L],half))
                if half==0: dq[rows,L]=g
                else: dq[rows,L]+=g
                grk[w,L]+=tdot(u,qb)
                return c
            lax.fori_loop(0,nb,qb_body,0,unroll=True)
            qh=only(q[:,L],half); dh=only(dctx[:,L],half)
            def kb_body(J,c):
                r0=pl.multiple_of(J*BLK,BLK)
                rows=pl.ds(r0,BLK)
                kb=only(k[rows,L],half)
                dt=ds[:,rows].T
                u=unskew(dt)
                w=pl.ds(r0,win)
                g=dot(dt,qh)+dot(u,only(rqs[w,L],half))
                gv=tdot(P[h,:,rows].astype(BF),dh)
                if half==0: dk[rows,L]=g; dv[rows,L]=gv
                else: dk[rows,L]+=g; dv[rows,L]+=gv
                grq[w,L]+=tdot(u,kb)
                return c
            lax.fori_loop(0,nb,kb_body,0,unroll=True)


EPS = 1e-07
HEADS = 16

def col_sum(x):
    return jnp.sum(x.astype(F32), axis=0)

def normalize(values_in, gain_row, shift_row):
    row_mean = jnp.mean(values_in, axis=-1, keepdims=True)
    centred = values_in - row_mean
    row_var = jnp.mean(centred * centred, axis=-1, keepdims=True)
    return centred * lax.rsqrt(row_var + EPS) * gain_row + shift_row

V = pl.BlockSpec(memory_space=pltpu.VMEM)
S = pl.BlockSpec(memory_space=pltpu.SMEM)
PARAMS = pltpu.CompilerParams(vmem_limit_bytes=48 * 2**20)

def fwd_kernel(scale, len_ref, q, k, v, rkf, rqf, ctx, P, across):
    slots, cols = q.shape
    attn_fwd(q, k, v, rkf, rqf, P, across, ctx, len_ref[0], slots, cols, scale)

def bwd_kernel(scale, q, k, v, dctx, rks, rqs, P, dq, dk, dv, grk, grq, ds):
    slots, cols = q.shape
    attn_bwd(q, k, v, dctx, rks, rqs, P, ds, dq, dk, dv, grk, grq, slots, cols, scale)

def per_device(hidden, lengths, buckets, w_query, w_key, w_value, w_output, b_query, b_key, b_value, b_output,
               rel_table, gain_attn, shift_attn, w_inner, b_inner, w_outer, b_outer, gain_ffn, shift_ffn, cotangent):
    nw = lax.axis_size("wt"); nc = lax.axis_size("ctx"); nd = lax.axis_size("dp")
    group = ("dp", "ctx"); ng = nd * nc
    tokens = hidden[0]
    rows, D = tokens.shape
    slots = rows * nc
    cols = D // nw
    wi = lax.axis_index("wt"); ci = lax.axis_index("ctx")
    scale = 1.0 / math.sqrt(3 * HD)
    a2a = lambda x, ax, s, c: lax.all_to_all(x, ax, split_axis=s, concat_axis=c, tiled=True)
    ag = lambda x: lax.all_gather(x, "wt", axis=0, tiled=True)
    rs = lambda x: lax.psum_scatter(x.astype(BF), "wt", scatter_dimension=0, tiled=True).astype(F32)
    tok_all = ag(tokens)
    rel_all = ag(rel_table)
    wqkv = jnp.concatenate([w_query.reshape(cols, nw, cols), w_key.reshape(cols, nw, cols), w_value.reshape(cols, nw, cols)], axis=2)
    wqkv = a2a(wqkv.reshape(cols, nw * 3 * cols), "wt", 1, 0)
    win_c = a2a(w_inner, "wt", 1, 0)
    cut = lambda b, n: lax.dynamic_slice_in_dim(b, wi * n, n)
    bq, bk, bv = cut(b_query, cols), cut(b_key, cols), cut(b_value, cols)
    wq_c, wk_c, wv_c = wqkv[:, :cols], wqkv[:, cols:2*cols], wqkv[:, 2*cols:]
    qkv = (dot(tok_all, wqkv) + jnp.concatenate([bq, bk, bv])).astype(BF)
    qkv = a2a(qkv, "ctx", 0, 0)
    q, k, v = qkv[:, :cols], qkv[:, cols:2*cols], qkv[:, 2*cols:]
    rk = (dot(rel_all, wk_c) + bk).astype(BF)
    rq = (dot(rel_all, wq_c) + bq).astype(BF)
    nb = rk.shape[0]
    pad = jnp.full((2 * slots - buckets.shape[0],), -1, jnp.int32)
    bs = jnp.concatenate([buckets, pad]); bf_ = jnp.concatenate([buckets[::-1], pad])
    ids = jnp.arange(nb, dtype=jnp.int32)
    hot_s = (bs[:, None] == ids[None, :]).astype(BF); hot_f = (bf_[:, None] == ids[None, :]).astype(BF)
    rr = jnp.concatenate([rk, rq], axis=1)
    rf = dot(hot_f, rr).astype(BF); rsn = dot(hot_s, rr).astype(BF)
    length = lax.dynamic_slice_in_dim(lax.all_gather(lengths, "wt", axis=0, tiled=True), ci, 1)
    ctx, P = pl.pallas_call(functools.partial(fwd_kernel, scale), name="attn_forward",
        out_shape=[jax.ShapeDtypeStruct((slots, cols), BF), jax.ShapeDtypeStruct((cols // HD, slots, slots), F32)],
        in_specs=[S] + [V] * 5, out_specs=[V, V], scratch_shapes=[pltpu.VMEM((slots, slots), F32)], compiler_params=PARAMS,
    )(length, q, k, v, rf[:, :cols], rf[:, cols:])
    ctx4 = a2a(ctx, "ctx", 0, 0)
    res_one = tokens.astype(F32) + rs(dot(ctx4, w_output)) + b_output
    normed = normalize(res_one, gain_attn, shift_attn)
    nl_all = ag(normed.astype(BF))
    inner_pre = dot(nl_all, win_c) + cut(b_inner, win_c.shape[1])
    active = jax.nn.gelu(inner_pre, approximate=False).astype(BF)
    res_two = normed + rs(dot(active, w_outer)) + b_outer
    result = normalize(res_two, gain_ffn, shift_ffn)
    pos = ci * rows + jnp.arange(rows, dtype=jnp.int32)
    seed = cotangent[0].astype(F32) * (pos < lengths[0]).astype(F32)[:, None]
    d_res_two, g_gain_ffn, g_shift_ffn = jax.vjp(normalize, res_two, gain_ffn, shift_ffn)[1](seed)
    db_all = ag(d_res_two.astype(BF))
    d_active = dot_t(db_all, w_outer)
    d_inner = jax.vjp(functools.partial(jax.nn.gelu, approximate=False), inner_pre)[1](d_active)[0].astype(BF)
    g_outer = tdot(active, db_all)
    g_inner = tdot(nl_all, d_inner)
    d_normed = d_res_two + rs(dot_t(d_inner, win_c))
    d_res_one, g_gain_attn, g_shift_attn = jax.vjp(normalize, res_one, gain_attn, shift_attn)[1](d_normed)
    da_all = ag(d_res_one.astype(BF))
    g_output = tdot(ctx4, da_all)
    dctx = a2a(dot_t(da_all, w_output).astype(BF), "ctx", 0, 0)
    dq, dk, dv, grk, grq = pl.pallas_call(functools.partial(bwd_kernel, scale), name="attn_backward",
        out_shape=[jax.ShapeDtypeStruct((slots, cols), F32)] * 3 + [jax.ShapeDtypeStruct((2 * slots, cols), F32)] * 2,
        in_specs=[V] * 7, out_specs=[V] * 5, scratch_shapes=[pltpu.VMEM((slots, slots), BF)], compiler_params=PARAMS,
    )(q, k, v, dctx, rsn[:, :cols], rsn[:, cols:], P)
    d4 = a2a(jnp.concatenate([dq, dk, dv], axis=1).astype(BF), "ctx", 0, 0)
    grr = tdot(hot_s, jnp.concatenate([grk, grq], axis=1).astype(BF)).astype(BF)
    grk_b, grq_b = grr[:, :cols], grr[:, cols:]
    g_qkv = tdot(tok_all, d4) + tdot(rel_all, jnp.concatenate([grq_b, grk_b, jnp.zeros_like(grk_b)], axis=1))
    g_rel = rs(dot_t(grk_b, wk_c) + dot_t(grq_b, wq_c))
    grad_tokens = d_res_one + rs(dot_t(d4, wqkv))
    by_rows = jnp.concatenate([g_outer, g_output, g_rel], axis=0).astype(BF)
    def by_group(g):
        n = g.shape[0] // (nw * ng)
        return g.astype(BF).reshape(nw, ng, n, g.shape[1]).transpose(1, 0, 2, 3).reshape(ng * nw * n, g.shape[1])
    by_cols = jnp.concatenate([by_group(g_inner), by_group(g_qkv)], axis=1)
    scat = lambda x: lax.psum_scatter(x, group, scatter_dimension=0, tiled=True)
    gat = lambda x: lax.all_gather(x, group, axis=0, tiled=True)
    row_part = gat(scat(by_rows)).astype(F32)
    mine = scat(by_cols)
    mine = a2a(mine, "wt", 0, 1)
    col_part = gat(mine).astype(F32)
    n_in = g_inner.shape[1]
    width = n_in + 3 * cols
    col_part = col_part.reshape(cols, nw, width)
    gi = col_part[:, :, :n_in].reshape(cols, nw * n_in)
    pick = lambda i: col_part[:, :, n_in + i * cols: n_in + (i + 1) * cols].reshape(cols, nw * cols)
    small_sh = jnp.concatenate([col_sum(d4) + jnp.concatenate([col_sum(grq_b), col_sum(grk_b), jnp.zeros((cols,), F32)]), col_sum(d_inner)])
    small_sh = lax.psum(small_sh, group)
    small = lax.psum(jnp.concatenate([col_sum(d_res_one.astype(BF)), col_sum(d_res_two.astype(BF)), g_gain_attn, g_shift_attn, g_gain_ffn, g_shift_ffn]), ("dp", "ctx", "wt"))
    sm = lambda i: cut(small[i * D:(i + 1) * D], cols)
    nf = g_outer.shape[0]
    return (result.astype(BF)[None], grad_tokens.astype(BF)[None], pick(0), pick(1), pick(2), row_part[nf:nf + cols],
        small_sh[:cols], small_sh[cols:2 * cols], small_sh[2 * cols:3 * cols], sm(0), row_part[nf + cols:], sm(2), sm(3),
        gi, small_sh[3 * cols:], row_part[:nf], sm(1), sm(4), sm(5))

def solution(mesh):
    in_specs = (
        P_(("dp", "wt"), "ctx", None),
        P_(("dp", "wt")),
        P_(),
        P_("wt", None),
        P_("wt", None),
        P_("wt", None),
        P_("wt", None),
        P_(),
        P_(),
        P_(),
        P_(),
        P_("wt", None),
        P_(),
        P_(),
        P_("wt", None),
        P_(),
        P_("wt", None),
        P_(),
        P_(),
        P_(),
        P_(("dp", "wt"), "ctx", None),
    )
    out_specs = (
        P_(("dp", "wt"), "ctx", None),
        P_(("dp", "wt"), "ctx", None),
        P_("wt", None),
        P_("wt", None),
        P_("wt", None),
        P_("wt", None),
        P_("wt"),
        P_("wt"),
        P_("wt"),
        P_("wt"),
        P_("wt", None),
        P_("wt"),
        P_("wt"),
        P_("wt", None),
        P_("wt"),
        P_("wt", None),
        P_("wt"),
        P_("wt"),
        P_("wt"),
    )
    return jax.shard_map(
        per_device, mesh=mesh, in_specs=in_specs, out_specs=out_specs, check_vma=False
    )
```

time: 1280 us -> 691 us (0.54)
  blocking collectives: 603 us -> 89.3 us
  local copies, waits for them, and re-layouts: 262 us -> 69.5 us
  waiting for transfers between devices: 241 us -> 387 us
  matrix products: 134 us -> 46.8 us
  Pallas kernels: 0 us -> 30.6 us
  starting transfers between devices: 0.85 us -> 23.8 us
    psum x2, blocking collectives: 592 us -> 62.4 us  [the longest x1 40.7 us: per_device(): lax.psum(jnp.concatenate([col_sum(d_res_one.astype(BF)), col_sum(d_res_tw...]
    reshape x10 -> x2, local copies, waits for them, and re-layouts: 168 us -> 9.67 us  [the longest x1 8.18 us: per_device(): col_part = col_part.reshape(cols, nw, width)]
    dot_general x37 -> x20, matrix products: 125 us -> 46.8 us  [the longest x8 20.9 us: dot(): return jnp.dot(a, b, preferred_element_type=F32)]
    all_to_all x0 -> x5, waiting for transfers between devices: none -> 76.5 us  [per_device(): lax.all_to_all(x, ax, split_axis=s, concat_axis=c, tiled=True)]
    reduce_scatter x6 -> x7, waiting for transfers between devices: 140 us -> 202 us  [the longest x2 113 us: per_device(): scat = lambda x: lax.psum_scatter(x, group, scatter_dimension=0, tiled=True)]
    pallas_call x0 -> x2, Pallas kernels: none -> 30.6 us  [the longest x1 17.3 us: per_device(): pl.pallas_call(functools.partial(bwd_kernel, scale), name='attn_backward'...]
    pad x4 -> x0, local copies, waits for them, and re-layouts: 23.8 us -> none  [the longest x2 15 us: unskew(): flat = jnp.pad(flat, ((0, 0), (row_count - 1, 1)))]
    all_to_all x0 -> x5, starting transfers between devices: none -> 22.6 us  [per_device(): lax.all_to_all(x, ax, split_axis=s, concat_axis=c, tiled=True)]
  transfers between devices with their start and end apart: 17 -> 19, of which waited for: 8 -> 16; matrix products, arithmetic and copies ran while one was open for 22% -> 11% of each run, Pallas kernels for 0% -> 0%
where the time goes in v1:
time: 691 us; the launch traced here: 686 us
  waiting for transfers between devices  387 us (56%)
  blocking collectives  89.3 us (13%)
  local copies, waits for them, and re-layouts  69.5 us (10%)
  matrix products  46.8 us (7%)
  Pallas kernels  30.6 us (4%)
  starting transfers between devices  23.8 us (3%)
  other arithmetic  23.4 us (3%)
  between operations  15.4 us (2%)
    reduce_scatter x2, waiting for transfers between devices, per_device(): scat = lambda x: lax.psum_scatter(x, group, scatter_dimension=0, tiled=True)  113 us
    reduce_scatter x5, waiting for transfers between devices, per_device(): lax.psum_scatter(x.astype(BF), 'wt', scatter_dimension=0, tiled=True)  89 us
    all_to_all x5, waiting for transfers between devices, per_device(): lax.all_to_all(x, ax, split_axis=s, concat_axis=c, tiled=True)  76.5 us
    all_gather x2, waiting for transfers between devices, per_device(): gat = lambda x: lax.all_gather(x, group, axis=0, tiled=True)  67.9 us
    psum x1, blocking collectives, per_device(): lax.psum(jnp.concatenate([col_sum(d_res_one.astype(BF)), col_sum(d_res_tw...  40.7 us
    all_gather x5, waiting for transfers between devices, per_device(): ag = lambda x: lax.all_gather(x, 'wt', axis=0, tiled=True)  39.7 us
    unnamed x100, local copies, waits for them, and re-layouts  27.7 us
    all_to_all x5, starting transfers between devices, per_device(): lax.all_to_all(x, ax, split_axis=s, concat_axis=c, tiled=True)  22.6 us
  transfers between devices with their start and end apart: 19, of which 16 were waited for; matrix products, arithmetic and copies ran while one was open for 11% of the time, Pallas kernels for 0%

profile of v1, /device:TPU:0, one launch (start us, length us, event | category | flops | bytes accessed | tf_op | source)
XLA Modules:
  0.0 686.1 jit_solution(12320794415619326873)
XLA Ops:
  10.4 2.0 copy.43
  12.5 2.3 pad_maximum_fusion.2
  14.8 4.4 all-to-all-start
  22.2 22.8 %all-to-all-done = bf16[256,4,768]{0,2,1:T(8,128)(2,1)} async-done(((bf16[256,4,768]{0,2,1:T(8,128)(2,1)}), bf16[256,4,768]{0,2,1:T(8,128)(2,1)}, u32[]{:S(2)}, u32[]{:S(2)}) %all-to-all-start) | async-done | bytes 1572896 | tf_op jit(solution)/shard_map/all_to_all | solution.py:145
  45.0 2.6 copy.46
  47.6 3.6 add_convert_fusion.3
  51.3 4.5 all-to-all-start.1
  57.7 4.5 all-reduce
  63.1 2.0 fusion.15
  65.1 1.6 fusion.16
  69.1 6.5 all-to-all-done.1
  78.8 13.3 %attn_forward.1 = (bf16[512,256]{1,0:T(8,128)(2,1)S(1)}, f32[4,512,512]{2,1,0:T(8,128)}) custom-call(s32[1]{0:T(128)} %dynamic_slice.33.len_ref, bf16[512,256]{1,0:T(8,128)(2,1)S(1)} %get-tuple-element.64.q, bf16[512,256]{1,0:T(8,128)(2,1)S(1)} %get-tuple-element.63.k, bf16[512,256]{1,0:T(8,128)(2,1)S(1)} %get-tuple-element.62.v, ...), custom_call_target="tpu_custom_call" | custom-call | tf_op jit(solution)/shard_map/attn_forward/pallas_call | solution.py:169
  92.1 10.7 %all_to_all.98 = bf16[4,128,256]{2,1,0:T(8,128)(2,1)S(1)} all-to-all(bf16[4,128,256]{2,1,0:T(8,128)(2,1)S(1)} %bitcast.110), channel_id=1, replica_groups=mesh['dp'=2,'ctx'=4,'wt'=4] {'ctx'}, dimensions={0} | all-to-all | bytes 524288 | tf_op jit(solution)/shard_map/all_to_all | solution.py:145
  103.5 1.4 convolution_convert_fusion.5
  105.0 4.1 copy.47
  109.0 4.6 all-to-all-start.3
  113.7 20.3 %reduce-scatter.8.cloned.1.call-done = bf16[128,1024]{1,0:T(8,128)(2,1)} async-done(((bf16[512,1024]{1,0:T(8,128)(2,1)}), bf16[128,1024]{1,0:T(8,128)(2,1)}) %reduce-scatter.8.cloned.1.call-update) | async-done | bytes 262160 | tf_op jit(solution)/shard_map/reduce_scatter | solution.py:147
  136.3 1.8 fusion.45
  139.5 5.6 all-to-all-done.3
  145.0 4.0 copy.48
  149.1 6.0 all-gather.11.cloned.1.call-done
  155.1 8.5 %multiply_convert_fusion = (bf16[512,1024]{1,0:T(8,128)(2,1)S(1)}, f32[512,1024]{1,0:T(8,128)}, f32[512,1024]{1,0:T(8,128)}) fusion(f32[1024]{0:T(1024)S(1)} %dynamic_slice.37, bf16[512,1024]{1,0:T(8,128)(2,1)} %all-gather.11.cloned.1.call-done, bf16[1024,1024]{1,0:T(8,128)(2,1)} %bitcast.131), kind=kOutput, calls=%fused_computation.11 | convolution fusion | flops 1108344832 | bytes 8392704 | tf_op jit(solution)/shard_map/dot_general | solution.py:12
  164.6 2.2 convolution_convert_fusion.4
  166.9 25.0 %reduce-scatter.10.cloned.1.call-done = bf16[128,1024]{1,0:T(8,128)(2,1)} async-done(((bf16[512,1024]{1,0:T(8,128)(2,1)}), bf16[128,1024]{1,0:T(8,128)(2,1)}) %reduce-scatter.10.cloned.1.call-update) | async-done | bytes 262160 | tf_op jit(solution)/shard_map/reduce_scatter | solution.py:147
  191.9 1.3 fusion.60
  193.4 1.3 fusion.36
  197.4 16.8 %all-gather.13.cloned.1.call-done = bf16[512,1024]{1,0:T(8,128)(2,1)} async-done(((bf16[128,1024]{1,0:T(8,128)(2,1)}), bf16[512,1024]{1,0:T(8,128)(2,1)}) %all-gather.13.cloned.1.call-update) | async-done | bytes 1048592 | tf_op jit(solution)/shard_map/all_gather | solution.py:146
  214.3 4.6 convert_reduce_fusion
  219.9 2.3 convolution_convert_fusion.3
  222.2 25.0 %reduce-scatter.12.cloned.1.call-done = bf16[128,1024]{1,0:T(8,128)(2,1)} async-done(((bf16[512,1024]{1,0:T(8,128)(2,1)}), bf16[128,1024]{1,0:T(8,128)(2,1)}) %reduce-scatter.12.cloned.1.call-update) | async-done | bytes 262160 | tf_op jit(solution)/shard_map/reduce_scatter | solution.py:147
  247.2 1.3 multiply_reduce_fusion
  248.5 1.3 fusion.58
  250.7 16.9 %all-gather.15.cloned.1.call-done = bf16[512,1024]{1,0:T(8,128)(2,1)} async-done(((bf16[128,1024]{1,0:T(8,128)(2,1)}), bf16[512,1024]{1,0:T(8,128)(2,1)}) %all-gather.15.cloned.1.call-update) | async-done | bytes 1048592 | tf_op jit(solution)/shard_map/all_gather | solution.py:146
  267.7 2.4 convolution_convert_fusion.7
  270.1 4.6 all-to-all-start.4
  275.7 8.3 %all-to-all-done.4 = bf16[4,128,256]{2,1,0:T(8,128)(2,1)S(1)} async-done(((bf16[4,128,256]{2,1,0:T(8,128)(2,1)}), bf16[4,128,256]{2,1,0:T(8,128)(2,1)S(1)}, u32[]{:S(2)}, u32[]{:S(2)}) %all-to-all-start.4) | async-done | bytes 262176 | tf_op jit(solution)/shard_map/all_to_all | solution.py:145
  284.0 17.3 %attn_backward.1 = (f32[512,256]{1,0:T(8,128)S(1)}, f32[512,256]{1,0:T(8,128)S(1)}, f32[512,256]{1,0:T(8,128)S(1)}, f32[1024,256]{1,0:T(8,128)S(1)}, f32[1024,256]{1,0:T(8,128)S(1)}) custom-call(bf16[512,256]{1,0:T(8,128)(2,1)S(1)} %get-tuple-element.64.q, bf16[512,256]{1,0:T(8,128)(2,1)S(1)} %get-tuple-element.63.k, ...), custom_call_target="tpu_custom_call" | custom-call | tf_op jit(solution)/shard_map/attn_backward/pallas_call | solution.py:194
  303.3 1.5 add_convert_fusion.1
  304.9 3.9 convolution_convert_fusion
  309.3 18.7 %reduce-scatter.18.cloned.1.call-done = bf16[128,1024]{1,0:T(8,128)(2,1)} async-done(((bf16[512,1024]{1,0:T(8,128)(2,1)}), bf16[128,1024]{1,0:T(8,128)(2,1)}) %reduce-scatter.18.cloned.1.call-update) | async-done | bytes 262160 | tf_op jit(solution)/shard_map/reduce_scatter | solution.py:147
  328.0 3.5 pad_maximum_fusion.1
  333.6 4.6 all-to-all-start.5
  338.2 2.7 convolution_convert_fusion.1
  340.9 1.5 copy.49
  342.5 33.3 %all-to-all-done.5 = bf16[4,128,768]{2,1,0:T(8,128)(2,1)S(1)} async-done(((bf16[4,128,768]{2,1,0:T(8,128)(2,1)}), bf16[4,128,768]{2,1,0:T(8,128)(2,1)S(1)}, u32[]{:S(2)}, u32[]{:S(2)}) %all-to-all-start.5) | async-done | bytes 786464 | tf_op jit(solution)/shard_map/all_to_all | solution.py:145
  377.0 2.2 fusion.11
  379.2 2.6 copy.50
  381.8 1.7 copy.51
  383.9 2.1 pad_maximum_fusion
  386.1 3.4 convolution_convert_fusion.2
  389.6 28.6 %reduce-scatter.20.cloned.1.call-done = bf16[176,1024]{1,0:T(8,128)(2,1)} async-done(((bf16[1408,1024]{1,0:T(8,128)(2,1)}), bf16[176,1024]{1,0:T(8,128)(2,1)}) %reduce-scatter.20.cloned.1.call-update) | async-done | bytes 360464 | tf_op jit(solution)/shard_map/reduce_scatter | solution.py:209
  418.3 84.1 %reduce-scatter.16.cloned.1.call-done = bf16[128,1792]{1,0:T(8,128)(2,1)} async-done(((bf16[1024,1792]{1,0:T(8,128)(2,1)}), bf16[128,1792]{1,0:T(8,128)(2,1)}) %reduce-scatter.16.cloned.1.call-update) | async-done | bytes 458768 | tf_op jit(solution)/shard_map/reduce_scatter | solution.py:209
  502.4 11.6 %all_to_all.99 = bf16[4,32,1792]{2,1,0:T(8,128)(2,1)S(1)} all-to-all(bf16[4,32,1792]{2,1,0:T(8,128)(2,1)} %bitcast.146), channel_id=1, replica_groups=mesh['dp'=2,'ctx'=4,'wt'=4] {'wt'}, dimensions={0} | all-to-all | bytes 917504 | tf_op jit(solution)/shard_map/all_to_all | solution.py:145
  514.8 40.7 %psum.15 = f32[6144]{0:T(1024)S(1)} all-reduce(f32[6144]{0:T(1024)S(1)} %constant_dynamic-update-slice_fusion), channel_id=1, replica_groups=mesh['dp'=2,'ctx'=4,'wt'=4] {'dp','ctx','wt'}, use_global_device_ids=true, to_apply=%region_26.0 | all-reduce | flops 6144 | bytes 49152 | tf_op jit(solution)/shard_map/psum | solution.py:222
  559.6 21.7 %psum.14 = f32[1792]{0:T(1024)S(1)} all-reduce(f32[1792]{0:T(1024)S(1)} %pad_maximum_fusion.7), channel_id=1, replica_groups=mesh['dp'=2,'ctx'=4,'wt'=4] {'dp','ctx'}, use_global_device_ids=true, to_apply=%region_19.0 | all-reduce | flops 1792 | bytes 14336 | tf_op jit(solution)/shard_map/psum | solution.py:221
  582.5 1.8 fusion.48
  584.3 5.5 all-gather.19.cloned.1.call-done
  589.8 2.3 slice.126
  592.1 1.8 slice.131
  593.9 2.5 slice.136
  596.4 62.4 %all-gather.17.cloned.1.call-done = bf16[256,7168]{1,0:T(8,128)(2,1)} async-done(((bf16[32,7168]{1,0:T(8,128)(2,1)}), bf16[256,7168]{1,0:T(8,128)(2,1)}) %all-gather.17.cloned.1.call-update) | async-done | bytes 3670032 | tf_op jit(solution)/shard_map/all_gather | solution.py:210
  658.8 8.2 %reshape.197 = f32[256,4,1792]{2,1,0:T(4,128)} reshape(bf16[256,7168]{1,0:T(8,128)(2,1)} %all-gather.17.cloned.1.call-done) | data formatting | bytes 11010048 | tf_op jit(solution)/shard_map/reshape | solution.py:217
  667.0 2.4 fusion.62
  673.5 5.8 copy.57
  (186 shorter events, 41.7 us)
Async XLA Ops:
  7.2 157.4 %copy-start = (bf16[1024,1024]{1,0:T(8,128)(2,1)S(1)}, bf16[1024,1024]{1,0:T(8,128)(2,1)}, u32[]{:S(2)}) copy-start(bf16[1024,1024]{1,0:T(8,128)(2,1)} %param.37) | copy-start | bytes 6291460
  7.2 40.4 %all-gather.21.cloned.1.call-start = ((), (), s32[]{:S(2)}) async-start(), calls=%async_computation.27 | async-start | bytes 1310720 | tf_op jit(solution)/shard_map/all_gather | solution.py:146
  14.8 30.2 %all-to-all-start = ((bf16[256,4,768]{0,2,1:T(8,128)(2,1)}), bf16[256,4,768]{0,2,1:T(8,128)(2,1)}, u32[]{:S(2)}, u32[]{:S(2)}) async-start(bf16[256,4,768]{0,2,1:T(8,128)(2,1)} %pad_maximum_fusion.2), calls=%async_computation | async-start | bytes 3145728 | tf_op jit(solution)/shard_map/all_to_all | solution.py:145
  19.1 44.0 %all-gather.9.cloned.1.call-start = ((), (), s32[]{:S(2)}) async-start(), calls=%async_computation.14 | async-start | bytes 1310720 | tf_op jit(solution)/shard_map/all_gather | solution.py:146
  47.6 8.8 %copy-start.34 = (u32[32]{0:T(128)S(1)}, u32[32]{0:T(128)}, u32[]{:S(2)}) copy-start(u32[32]{0:T(128)} %constant.106) | copy-start | bytes 388
  47.6 14.7 %copy-start.29 = (s32[1023]{0:T(1024)S(1)}, s32[1023]{0:T(1024)}, u32[]{:S(2)}) copy-start(s32[1023]{0:T(1024)} %param.23) | copy-start | bytes 12280
  51.3 24.3 %all-to-all-start.1 = ((bf16[4,128,768]{2,1,0:T(8,128)(2,1)}), bf16[4,128,768]{2,1,0:T(8,128)(2,1)S(1)}, u32[]{:S(2)}, u32[]{:S(2)}) async-start(bf16[4,128,768]{2,1,0:T(8,128)(2,1)} %bitcast.145), calls=%async_computation.1 | async-start | bytes 1572864 | tf_op jit(solution)/shard_map/all_to_all | solution.py:145
  55.7 78.3 %reduce-scatter.8.cloned.1.call-start = ((), (), s32[]{:S(2)}) async-start(), calls=%async_computation.15 | async-start | bytes 1310720 | tf_op jit(solution)/shard_map/reduce_scatter | solution.py:147
  63.1 2.0 copy-start.21
  65.1 1.6 copy-start.35
  66.7 0.7 copy-start.37
  75.6 0.9 copy-start.14
  76.5 27.0 %copy-start.23 = (bf16[256,1024]{1,0:T(8,128)(2,1)S(1)}, bf16[256,1024]{1,0:T(8,128)(2,1)}, u32[]{:S(2)}) copy-start(bf16[256,1024]{1,0:T(8,128)(2,1)} %param.27) | copy-start | bytes 1572868
  77.7 1.0 copy-start.2
  102.8 0.7 copy-start.15
  109.0 25.0 %copy-start.5 = (bf16[1,128,1024]{2,1,0:T(8,128)(2,1)S(1)}, bf16[1,128,1024]{2,1,0:T(8,128)(2,1)}, u32[]{:S(2)}) copy-start(bf16[1,128,1024]{2,1,0:T(8,128)(2,1)} %param.21) | copy-start | bytes 786436
  109.0 25.0 %copy-start.25 = (f32[1024]{0:T(1024)S(1)}, f32[1024]{0:T(1024)}, u32[]{:S(2)}) copy-start(f32[1024]{0:T(1024)} %param.31) | copy-start | bytes 12292
  109.0 27.3 %copy-start.26 = (f32[1024]{0:T(1024)S(1)}, f32[1024]{0:T(1024)}, u32[]{:S(2)}) copy-start(f32[1024]{0:T(1024)} %param.33) | copy-start | bytes 12292
  109.0 27.3 %copy-start.27 = (f32[1024]{0:T(1024)S(1)}, f32[1024]{0:T(1024)}, u32[]{:S(2)}) copy-start(f32[1024]{0:T(1024)} %param.34) | copy-start | bytes 12292
  109.0 36.0 %all-to-all-start.3 = ((bf16[256,4,1024]{0,2,1:T(8,128)(2,1)}), bf16[256,4,1024]{0,2,1:T(8,128)(2,1)}, u32[]{:S(2)}, u32[]{:S(2)}) async-start(bf16[256,4,1024]{0,2,1:T(8,128)(2,1)} %bitcast.115), calls=%async_computation.4 | async-start | bytes 4194304 | tf_op jit(solution)/shard_map/all_to_all | solution.py:145
  113.7 41.4 %all-gather.11.cloned.1.call-start = ((), (), s32[]{:S(2)}) async-start(), calls=%async_computation.16 | async-start | bytes 1310720 | tf_op jit(solution)/shard_map/all_gather | solution.py:146
  138.2 53.7 %reduce-scatter.10.cloned.1.call-start = ((), (), s32[]{:S(2)}) async-start(), calls=%async_computation.17 | async-start | bytes 1310720 | tf_op jit(solution)/shard_map/reduce_scatter | solution.py:147
  163.6 1.0 copy-start.39
  164.6 27.3 %copy-start.7 = (bf16[128,1024]{1,0:T(8,128)(2,1)S(1)}, bf16[128,1024]{1,0:T(8,128)(2,1)}, u32[]{:S(2)}) copy-start(bf16[128,1024]{1,0:T(8,128)(2,1)} %reduce-scatter.8.cloned.1.call-done) | copy-start | bytes 786436
  164.6 27.3 %copy-start.30 = (f32[1024]{0:T(1024)S(1)}, f32[1024]{0:T(1024)}, u32[]{:S(2)}) copy-start(f32[1024]{0:T(1024)} %param.38) | copy-start | bytes 12292
  166.8 26.6 %copy-start.28 = (f32[1024]{0:T(1024)S(1)}, f32[1024]{0:T(1024)}, u32[]{:S(2)}) copy-start(f32[1024]{0:T(1024)} %param.39) | copy-start | bytes 12292
  166.8 27.9 %copy-start.31 = (f32[1024]{0:T(1024)S(1)}, f32[1024]{0:T(1024)}, u32[]{:S(2)}) copy-start(f32[1024]{0:T(1024)} %param.40) | copy-start | bytes 12292
  166.8 47.4 %all-gather.13.cloned.1.call-start = ((), (), s32[]{:S(2)}) async-start(), calls=%async_computation.18 | async-start | bytes 1310720 | tf_op jit(solution)/shard_map/all_gather | solution.py:146
  191.9 2.8 copy-start.19
  195.7 0.8 copy-start.9
  197.4 49.8 %reduce-scatter.12.cloned.1.call-start = ((), (), s32[]{:S(2)}) async-start(), calls=%async_computation.19 | async-start | bytes 1310720 | tf_op jit(solution)/shard_map/reduce_scatter | solution.py:147
  214.3 5.6 copy-start.17
  218.9 1.0 copy-start.40
  219.9 27.3 %copy-start.10 = (f32[128,1024]{1,0:T(8,128)S(1)}, f32[128,1024]{1,0:T(8,128)}, u32[]{:S(2)}) copy-start(f32[128,1024]{1,0:T(8,128)} %copy-done.9) | copy-start | bytes 1572868
  222.2 45.5 %copy-start.24 = (bf16[256,1024]{1,0:T(8,128)(2,1)S(1)}, bf16[256,1024]{1,0:T(8,128)(2,1)}, u32[]{:S(2)}) copy-start(bf16[256,1024]{1,0:T(8,128)(2,1)} %param.27) | copy-start | bytes 1572868
  222.2 45.5 %all-gather.15.cloned.1.call-start = ((), (), s32[]{:S(2)}) async-start(), calls=%async_computation.20 | async-start | bytes 1310720 | tf_op jit(solution)/shard_map/all_gather | solution.py:146
  249.9 25.8 %copy-start.11 = (f32[128,1024]{1,0:T(8,128)}, f32[128,1024]{1,0:T(8,128)S(1)}, u32[]{:S(2)}) copy-start(f32[128,1024]{1,0:T(8,128)S(1)} %get-tuple-element.48) | copy-start | bytes 1572868
  249.9 25.0 %copy-start.36 = (bf16[512,256]{0,1:T(8,128)(2,1)S(1)}, bf16[512,256]{0,1:T(8,128)(2,1)}, u32[]{:S(2)}) copy-start(bf16[512,256]{0,1:T(8,128)(2,1)} %copy-done.35) | copy-start | bytes 786436
  249.9 25.0 %copy-start.38 = (bf16[512,256]{0,1:T(8,128)(2,1)S(1)}, bf16[512,256]{0,1:T(8,128)(2,1)}, u32[]{:S(2)}) copy-start(bf16[512,256]{0,1:T(8,128)(2,1)} %copy-done.37) | copy-start | bytes 786436
  270.1 13.9 %all-to-all-start.4 = ((bf16[4,128,256]{2,1,0:T(8,128)(2,1)}), bf16[4,128,256]{2,1,0:T(8,128)(2,1)S(1)}, u32[]{:S(2)}, u32[]{:S(2)}) async-start(bf16[4,128,256]{2,1,0:T(8,128)(2,1)} %bitcast.21), calls=%async_computation.7 | async-start | bytes 524288 | tf_op jit(solution)/shard_map/all_to_all | solution.py:145
  274.7 53.3 %reduce-scatter.18.cloned.1.call-start = ((), (), s32[]{:S(2)}) async-start(), calls=%async_computation.24 | async-start | bytes 1310720 | tf_op jit(solution)/shard_map/reduce_scatter | solution.py:147
  301.3 1.2 copy-start.3
  301.4 1.5 copy-start.13
  303.3 1.6 copy-start.33
  304.8 4.0 copy-start.16
  304.8 113.3 %reduce-scatter.20.cloned.1.call-start = ((), (), s32[]{:S(2)}) async-start(), calls=%async_computation.25 | async-start | bytes 3244032 | tf_op jit(solution)/shard_map/reduce_scatter | solution.py:209
  304.9 3.9 copy-start.18
  331.5 1.0 copy-start.4
  332.6 5.6 copy-start.32
  333.6 42.2 %all-to-all-start.5 = ((bf16[4,128,768]{2,1,0:T(8,128)(2,1)}), bf16[4,128,768]{2,1,0:T(8,128)(2,1)S(1)}, u32[]{:S(2)}, u32[]{:S(2)}) async-start(bf16[4,128,768]{2,1,0:T(8,128)(2,1)} %pad_maximum_fusion.3), calls=%async_computation.8 | async-start | bytes 1572864 | tf_op jit(solution)/shard_map/all_to_all | solution.py:145
  338.2 164.2 %reduce-scatter.16.cloned.1.call-start = ((), (), s32[]{:S(2)}) async-start(), calls=%async_computation.22 | async-start | bytes 4128768 | tf_op jit(solution)/shard_map/reduce_scatter | solution.py:209
  340.9 34.8 %copy-start.20 = (bf16[1,512,1024]{2,1,0:T(8,128)(2,1)S(1)}, bf16[1,512,1024]{2,1,0:T(8,128)(2,1)}, u32[]{:S(2)}) copy-start(bf16[1,512,1024]{2,1,0:T(8,128)(2,1)} %all-gather.21.cloned.1.call-done) | copy-start | bytes 3145732
  375.7 1.2 copy-start.22
  381.8 2.1 copy-start.8
  386.1 196.5 %reduce-scatter.14.cloned.1.call-start = ((), (), s32[]{:S(2)}) async-start(), calls=%async_computation.21 | async-start | bytes 1310720 | tf_op jit(solution)/shard_map/reduce_scatter | solution.py:147
  389.5 200.3 %all-gather.19.cloned.1.call-start = ((), (), s32[]{:S(2)}) async-start(), calls=%async_computation.26 | async-start | bytes 3244032 | tf_op jit(solution)/shard_map/all_gather | solution.py:210
  418.2 164.4 %copy-start.12 = (f32[128,1024]{1,0:T(8,128)S(1)}, f32[128,1024]{1,0:T(8,128)}, u32[]{:S(2)}) copy-start(f32[128,1024]{1,0:T(8,128)} %copy-done.11) | copy-start | bytes 1572868
  418.2 240.6 %all-gather.17.cloned.1.call-start = ((), (), s32[]{:S(2)}) async-start(), calls=%async_computation.23 | async-start | bytes 4128768 | tf_op jit(solution)/shard_map/all_gather | solution.py:210
  589.8 4.1 copy-start.6
  670.6 2.9 slice-start
  673.5 5.8 copy-start.1
Sparse Core Ops, SparseCore 0:
  9.6 24.2 all-gather.20
  35.4 16.0 all-gather.8
  105.1 28.9 reduce-scatter.7
  138.3 16.7 all-gather.10
  166.9 24.8 reduce-scatter.9
  197.5 16.7 all-gather.12
  222.3 24.8 reduce-scatter.11
  250.9 16.7 all-gather.14
  304.9 22.9 reduce-scatter.17
  331.9 86.2 reduce-scatter.19
  422.4 79.9 reduce-scatter.15
  505.3 24.7 reduce-scatter.13
  532.4 57.3 all-gather.18
  592.6 66.1 all-gather.16
